TPU v7x, 512 devices: a whole 4x4x16 slice. The times are simulated.
512 devices in a mesh: row: 16 (over y, x_hi, core), col: 32 (over z, x_lo).
Axes of the slice: x: 4 (x_hi: 2, x_lo: 2; x = x_hi * 2 + x_lo), y: 4, z: 16, core: 2. Of those that a mesh axis runs over, the one named last changes fastest.
Arguments:
- hess_inv: float32 [16384, 16384], P('row', 'col'), as said below
- weights: bfloat16 [6144, 16384], P('row', 'col'), may hold values from -6 to 6
- removed: int32 [512], replicated, may hold values from 0 to 16383, as said below
Outputs:
- hess_out: float32 [16384, 16384], P('row', 'col')
- weight_out: bfloat16 [6144, 16384], P('row', 'col')
Inputs may be any that keep to these rules, and one draw needn't show every extreme that they name: `removed`: sorted ascending and distinct; each aligned block of 512 columns holds at most 48 of them, and at least one block holds exactly 48. `hess_inv`: symmetric and positive definite.
All inputs are finite; a program needn't handle non-finite values.
Results may differ from a plain program's by a relative error of at most 0.005.
Values may be sent and summed in bfloat16 or wider, within the bound.
A program may use at most 64 MiB of HBM per device.

v0:
```python
import jax
import jax.numpy as jnp
from jax import lax
from jax.sharding import PartitionSpec as P

MOST = 48


def spread(block, axis, owner):
    block = jnp.where(lax.axis_index(axis) == owner, block, jnp.zeros_like(block))
    return lax.psum(block, axis)


def pick_owned(source, removed, tile_index, tile_size, slot_count, which_axis):
    before = jnp.sum((removed < tile_index * tile_size).astype(jnp.int32))
    within = jnp.sum((removed // tile_size == tile_index).astype(jnp.int32))
    slot_rank = jnp.arange(slot_count, dtype=jnp.int32)
    chosen = jnp.clip(before + slot_rank, 0, removed.shape[0] - 1)
    local_col = jnp.clip(removed[chosen] - tile_index * tile_size, 0, tile_size - 1)
    taken_part = jnp.take(source, local_col, axis=which_axis)
    live_slot = slot_rank < within
    mask_shape = [1, 1]
    mask_shape[which_axis] = slot_count
    return jnp.where(live_slot.reshape(mask_shape), taken_part, jnp.zeros((), taken_part.dtype))


def slot_map(removed, tile_size, slot_count):
    which_tile = removed // tile_size
    first_pos = jnp.sum(
        (removed[None, :] < (which_tile * tile_size)[:, None]).astype(jnp.int32), axis=1
    )
    position = jnp.arange(removed.shape[0], dtype=jnp.int32)
    return which_tile * slot_count + position - first_pos


def on_device(hess_inv, weights, removed):
    row_count = lax.axis_size("row")
    col_count = lax.axis_size("col")
    col_index = lax.axis_index("col")
    row_tile, col_tile = hess_inv.shape
    tile_ratio = col_count // row_count
    col_slots = slot_map(removed, col_tile, MOST)
    packed_weight = pick_owned(weights, removed, col_index, col_tile, MOST, 1)
    packed_hess = pick_owned(hess_inv, removed, col_index, col_tile, MOST, 1)
    wide_hess, weight_wide = (
        lax.all_gather(packed_hess, "col", axis=1, tiled=True),
        lax.all_gather(packed_weight.astype(jnp.float32), "col", axis=1, tiled=True).astype(
            packed_weight.dtype
        ),
    )
    left_side = jnp.take(wide_hess, col_slots, axis=1)
    weight_left = jnp.take(weight_wide, col_slots, axis=1)
    mirror_part = lax.dynamic_slice_in_dim(
        left_side, col_index % tile_ratio * col_tile, col_tile, 0
    )
    mirrored = spread(mirror_part, "row", col_index // tile_ratio)
    upper_rows = mirrored.T
    own_cols = pick_owned(upper_rows, removed, col_index, col_tile, MOST, 1)
    block_wide = lax.all_gather(own_cols, "col", axis=1, tiled=True)
    removed_block = jnp.take(block_wide, col_slots, axis=1)
    factor = jnp.linalg.cholesky(removed_block)
    identity = jnp.eye(removed_block.shape[0], dtype=jnp.float32)
    factor_inv = jax.scipy.linalg.solve_triangular(factor, identity, lower=True)
    block_inv = jnp.dot(factor_inv.T, factor_inv, precision=lax.Precision.HIGHEST)
    coupling = jnp.dot(block_inv, upper_rows, precision=lax.Precision.HIGHEST)
    correction = jnp.dot(left_side, coupling, precision=lax.Precision.HIGHEST)
    hess_out = hess_inv - correction
    weight_fix = jnp.dot(weight_left.astype(jnp.float32), coupling, precision=lax.Precision.HIGHEST)
    weight_out = (weights.astype(jnp.float32) - weight_fix).astype(jnp.bfloat16)
    return (hess_out, weight_out)


def solution(mesh):
    placed = (P("row", "col"), P("row", "col"), P())
    return jax.shard_map(
        on_device,
        mesh=mesh,
        in_specs=placed,
        out_specs=(P("row", "col"), P("row", "col")),
        check_vma=False,
    )
```

profile of v0, /device:TPU:24, one launch (start us, length us, event | category | flops | bytes accessed | tf_op | source)
XLA Modules:
  0.0 811.0 jit_solution(553122249612259826)
XLA Ops:
  7.2 1.9 copy.13
  9.8 0.7 fusion.42
  10.5 0.8 gather_fusion
  11.9 0.7 compare_and_fusion
  12.6 0.6 gather_fusion.1
  13.2 0.8 select_bitcast_fusion.2
  14.4 161.2 %all-gather.4.cloned.1.call-done = f32[1024,1536]{0,1:T(8,128)} async-done(((f32[1024,48]{0,1:T(8,128)}), f32[1024,1536]{0,1:T(8,128)}) %all-gather.4.cloned.1.call-update) | async-done | bytes 6291472 | tf_op jit(solution)/shard_map/all_gather | solution.py:46
  175.6 6.4 gather_fusion.2
  182.0 1.8 broadcast_select_fusion
  183.8 1.1 select_bitcast_fusion
  185.2 0.7 gather_fusion.5
  185.9 0.7 convert_bitcast_fusion
  186.7 144.8 %all-reduce.3.cloned.1.call-done = f32[512,512]{0,1:T(8,128)} async-done(((f32[512,512]{0,1:T(8,128)}), f32[512,512]{0,1:T(8,128)}) %all-reduce.3.cloned.1.call-update) | async-done | bytes 1048592 | tf_op jit(solution)/shard_map/psum | solution.py:11
  331.4 1.6 copy.14
  333.6 0.7 select_bitcast_fusion.3
  334.9 0.8 iota_compare_fusion
  335.7 1.1 fusion.19
  336.8 136.2 %all-gather.8.cloned.1.call-done = bf16[384,1536]{0,1:T(8,128)(2,1)} async-done(((bf16[384,48]{0,1:T(8,128)(2,1)}), bf16[384,1536]{0,1:T(8,128)(2,1)}) %all-gather.8.cloned.1.call-update) | async-done | bytes 1179664 | tf_op jit(solution)/shard_map/all_gather | solution.py:47
  473.0 3.2 gather_fusion.6
  476.2 135.2 %all-gather.6.cloned.1.call-done = f32[512,1536]{0,1:T(8,128)} async-done(((f32[512,48]{0,1:T(8,128)}), f32[512,1536]{0,1:T(8,128)}) %all-gather.6.cloned.1.call-update) | async-done | bytes 3145744 | tf_op jit(solution)/shard_map/all_gather | solution.py:59
  611.4 4.4 gather_fusion.4
  615.8 1.1 select_bitcast_fusion.1
  616.9 2.5 copy.15
  619.5 1.4 add_multiply_fusion
  620.9 1.0 copy-done.4
  621.9 11.7 %cholesky.102 = f32[128,128]{1,0:T(8,128)S(1)} custom-call(f32[128,128]{1,0:T(8,128)S(1)} %cholesky.260), custom_call_target="Cholesky" | custom-call | tf_op jit(solution)/shard_map/jit(cholesky)/cholesky | solution.py:61
  634.9 1.0 cholesky.220
  635.8 11.3 %custom-call.31 = f32[1,128,128]{1,2,0:T(8,128)} custom-call(f32[1,128,128]{2,1,0:T(8,128)} %get-tuple-element.33), custom_call_target="InvertDiagBlocksLowerTriangular" | custom-call | tf_op jit(solution)/shard_map/jit(cholesky)/cholesky | solution.py:61
  647.1 1.2 constant_dynamic-update-slice_fusion.3
  648.3 1.3 convolution_subtract_fusion.5
  649.6 0.7 copy-done.7
  650.9 13.2 %cholesky.213 = f32[128,128]{1,0:T(8,128)} custom-call(f32[128,128]{1,0:T(8,128)} %cholesky.264), custom_call_target="Cholesky" | custom-call | tf_op jit(solution)/shard_map/jit(cholesky)/cholesky | solution.py:61
  664.1 1.5 select_reduce_fusion.2
  665.5 11.4 %custom-call.32 = f32[1,128,128]{1,2,0:T(8,128)} custom-call(f32[1,128,128]{2,1,0:T(8,128)} %get-tuple-element.30), custom_call_target="InvertDiagBlocksLowerTriangular" | custom-call | tf_op jit(solution)/shard_map/jit(cholesky)/cholesky | solution.py:61
  677.0 1.2 convolution_dynamic-update-slice_fusion
  678.1 1.3 convolution_subtract_fusion.6
  680.7 13.2 %cholesky.234 = f32[128,128]{1,0:T(8,128)} custom-call(f32[128,128]{1,0:T(8,128)} %cholesky.269), custom_call_target="Cholesky" | custom-call | tf_op jit(solution)/shard_map/jit(cholesky)/cholesky | solution.py:61
  693.9 1.5 select_reduce_fusion.1
  695.3 11.3 %custom-call.33 = f32[1,128,128]{1,2,0:T(8,128)} custom-call(f32[1,128,128]{2,1,0:T(8,128)} %get-tuple-element.27), custom_call_target="InvertDiagBlocksLowerTriangular" | custom-call | tf_op jit(solution)/shard_map/jit(cholesky)/cholesky | solution.py:61
  706.6 1.1 convolution_dynamic-update-slice_fusion.1
  707.7 1.8 convolution_subtract_fusion.7
  709.5 13.2 %cholesky.251 = f32[128,128]{1,0:T(8,128)} custom-call(f32[128,128]{1,0:T(8,128)} %convolution_subtract_fusion.7), custom_call_target="Cholesky" | custom-call | tf_op jit(solution)/shard_map/jit(cholesky)/cholesky | solution.py:61
  722.7 0.9 select_reduce_fusion
  723.6 0.6 compare_reduce_fusion.3
  724.2 0.7 compare_reduce_fusion.2
  724.9 0.7 compare_reduce_fusion.1
  725.6 0.9 compare_reduce_fusion
  729.1 1.1 select_select_fusion
  730.2 0.7 triangular_solve.97
  730.9 14.4 %while.1 = (s32[]{:T(128)}, f32[512,512]{1,0:T(8,128)}, s32[4,2]{0,1:T(2,128)S(1)}, f32[4,128,128]{2,1,0:T(8,128)}, s32[]{:T(128)}) while((s32[]{:T(128)}, f32[512,512]{1,0:T(8,128)}, s32[4,2]{0,1:T(2,128)S(1)}, f32[4,128,128]{2,1,0:T(8,128)}, s32[]{:T(128)}) %tuple.34), condition=%wide.while_cond, body=%wide.while_body.sunk | while | flops 2 | bytes 132205 | solution.py:63
  731.5 2.9 bitcast_dynamic-update-slice_fusion.2
  735.2 2.9 bitcast_dynamic-update-slice_fusion.2
  738.8 2.9 bitcast_dynamic-update-slice_fusion.2
  742.4 2.9 bitcast_dynamic-update-slice_fusion.2
  745.3 40.7 %custom-call.34 = f32[4,128,128]{1,2,0:T(8,128)} custom-call(f32[4,128,128]{2,1,0:T(8,128)} %get-tuple-element.9), custom_call_target="InvertDiagBlocksLowerTriangular" | custom-call | tf_op jit(solution)/shard_map/jit(_solve_triangular)/triangular_solve | solution.py:63
  786.0 1.2 fusion.21
  787.2 1.4 convolution_subtract_fusion.3
  788.6 1.3 fusion.34
  789.9 1.3 convolution_subtract_fusion.2
  791.7 1.7 convolution_subtract_fusion.4
  793.7 1.9 fusion.1
  795.7 1.9 fusion.49
  797.6 4.8 convolution_subtract_fusion
  802.4 1.8 fusion
  (54 shorter events, 9.8 us)
Async XLA Ops:
  7.2 168.5 %all-gather.4.cloned.1.call-start = ((), (), s32[]{:S(2)}) async-start(), calls=%async_computation | async-start | bytes 6488064 | tf_op jit(solution)/shard_map/all_gather | solution.py:46
  7.2 2.0 copy-start
  14.0 317.4 %all-reduce.3.cloned.1.call-start = ((), (), s32[]{:S(2)}) async-start(), calls=%async_computation.1 | async-start | bytes 2097152 | tf_op jit(solution)/shard_map/psum | solution.py:11
  183.8 1.2 copy-start.5
  185.0 288.0 %all-gather.8.cloned.1.call-start = ((), (), s32[]{:S(2)}) async-start(), calls=%async_computation.3 | async-start | bytes 1216512 | tf_op jit(solution)/shard_map/all_gather | solution.py:47
  186.6 424.8 %all-gather.6.cloned.1.call-start = ((), (), s32[]{:S(2)}) async-start(), calls=%async_computation.2 | async-start | bytes 3244032 | tf_op jit(solution)/shard_map/all_gather | solution.py:59
  620.9 1.0 copy-start.4
  633.6 0.6 copy-start.10
  649.6 0.7 copy-start.7
  679.4 0.6 copy-start.8
  730.2 59.7 %copy-start.3 = (f32[512,512]{1,0:T(8,128)S(1)}, f32[512,512]{1,0:T(8,128)}, u32[]{:S(2)}) copy-start(f32[512,512]{1,0:T(8,128)} %fusion.19) | copy-start | bytes 3145732
  786.0 5.2 copy-start.9
  791.6 4.0 copy-start.2
  795.7 1.9 copy-start.1
  797.6 4.8 copy-start.6
Sparse Core Ops, SparseCore 0:
  14.2 161.4 all-gather.3
  185.1 146.3 all-reduce.2
  333.7 139.2 all-gather.7
  475.7 135.6 all-gather.5
where the time goes:
time: 817 us; the launch traced here: 811 us
  waiting for transfers between devices  577 us (71%)
  other arithmetic  147 us (18%)
  local copies, waits for them, and re-layouts  43.2 us (5%)
  matrix products  25.9 us (3%)
  between operations  17 us (2%)
    all_gather x1, waiting for transfers between devices, on_device(): lax.all_gather(packed_hess, 'col', axis=1, tiled=True)  161 us
    psum x1, waiting for transfers between devices, spread(): return lax.psum(block, axis)  145 us
    all_gather x1, waiting for transfers between devices, on_device(): lax.all_gather(packed_weight.astype(jnp.float32), 'col', axis=1, tiled=True)  136 us
    all_gather x1, waiting for transfers between devices, on_device(): block_wide = lax.all_gather(own_cols, 'col', axis=1, tiled=True)  135 us
    another operation x15, other arithmetic, on_device(): factor = jnp.linalg.cholesky(removed_block)  92.5 us
    another operation x3, other arithmetic, on_device(): factor_inv = jax.scipy.linalg.solve_triangular(factor, identity, lower=True)  42.4 us
  transfers between devices with their start and end apart: 4, of which 4 were waited for; matrix products, arithmetic and copies ran while one was open for 1% of the time, Pallas kernels for 0%

commit v1 on v0

v1 whole, which is shorter than its diff:
```python
import functools

import jax
import jax.numpy as jnp
from jax import lax
from jax.experimental import pallas as pl
from jax.experimental.pallas import tpu as pltpu
from jax.sharding import PartitionSpec as P

MESH = pl.DeviceIdType.MESH
HIGHEST = lax.Precision.HIGHEST
LANES = 128


def all_bytes(ref, sem):
    return pltpu.make_async_copy(ref, ref, sem)


def exchange_kernel(
    rows,
    cols,
    hess_ref,
    weight_ref,
    rem_row_ref,
    rem_col_ref,
    block_ref,
    left_ref,
    upper_ref,
    wleft_ref,
    yt_ref,
    bp_ref,
    xh_ref,
    xw_ref,
    ra_ref,
    ru_ref,
    sb_ref,
    rb_ref,
    row_ref,
    rc_ref,
    rl_ref,
    rw_ref,
    send_sems,
    recv_sems,
    ring_send,
    ring_recv,
    wring_send,
    wring_recv,
):
    r = lax.axis_index("row")
    c = lax.axis_index("col")
    tall, wide = hess_ref.shape
    count = rem_col_ref.shape[0]
    groups = count // LANES
    share = count // rows
    zs = cols // 2
    wchunk = 16
    wowners = weight_ref.shape[0] // wchunk

    barrier = pltpu.get_barrier_semaphore()

    @pl.loop(1, rows)
    def _(k):
        pl.semaphore_signal(
            barrier, inc=1, device_id={"row": lax.rem(r + k, rows)}, device_id_type=MESH
        )

    @pl.loop(1, cols)
    def _(k):
        pl.semaphore_signal(
            barrier, inc=1, device_id={"col": lax.rem(c + k, cols)}, device_id_type=MESH
        )

    col_iota = lax.broadcasted_iota(jnp.int32, (wide, LANES), 0) + c * wide
    row_iota = lax.broadcasted_iota(jnp.int32, (LANES, tall), 1) + r * tall
    pick_col = jnp.zeros((wide, LANES), jnp.float32)
    pick_row = jnp.zeros((LANES, tall), jnp.float32)
    for g in range(groups):
        pick_col = jnp.where(rem_row_ref[g : g + 1, :] == col_iota, 1.0, pick_col)
        pick_row = jnp.where(
            rem_col_ref[g * LANES : (g + 1) * LANES, :] == row_iota, 1.0, pick_row
        )

    own_rows = jnp.dot(
        pick_row, hess_ref[...], precision=HIGHEST, preferred_element_type=jnp.float32
    )
    bp_ref[...] = jnp.dot(
        own_rows, pick_col, precision=HIGHEST, preferred_element_type=jnp.float32
    )
    pl.semaphore_wait(barrier, rows + cols - 2)

    def spread_rows(src, dst, which):
        @pl.loop(1, rows)
        def _(k):
            to = lax.rem(r + k, rows)
            pltpu.make_async_remote_copy(
                src_ref=src(to),
                dst_ref=dst,
                send_sem=send_sems.at[which],
                recv_sem=recv_sems.at[which],
                device_id={"row": to},
                device_id_type=MESH,
            ).start()

    def spread_cols(src, dst, which, limit):
        @pl.loop(1, cols)
        def _(k):
            to = lax.rem(c + k, cols)

            @pl.when(to < limit)
            def _():
                pltpu.make_async_remote_copy(
                    src_ref=src(to),
                    dst_ref=dst,
                    send_sem=send_sems.at[which],
                    recv_sem=recv_sems.at[which],
                    device_id={"col": to},
                    device_id_type=MESH,
                ).start()

    spread_rows(lambda to: bp_ref.at[pl.ds(lax.rem(to, 4) * share, share)], ra_ref.at[r], 0)
    ra_ref[r] = bp_ref[pl.ds(lax.rem(r, 4) * share, share), :]
    yt_ref[...] = own_rows.T
    spread_rows(lambda to: yt_ref.at[pl.ds(to * share, share)], ru_ref.at[r], 1)
    ru_ref[r] = yt_ref[pl.ds(r * share, share), :]

    xh_ref[...] = jnp.dot(
        hess_ref[...], pick_col, precision=HIGHEST, preferred_element_type=jnp.float32
    )
    xw_ref[...] = jnp.dot(
        weight_ref[...], pick_col.astype(jnp.bfloat16), preferred_element_type=jnp.float32
    ).astype(jnp.bfloat16)

    tile_row = [lax.shift_right_logical(rem_row_ref[g : g + 1, :], 9) for g in range(groups)]

    all_bytes(ra_ref.at[pl.ds(0, rows - 1)], recv_sems.at[0]).wait()
    own_src = lax.shift_right_logical(rem_col_ref[pl.ds(r * share, share), :], 10)
    strip = jnp.zeros((share, LANES), jnp.float32)
    for k in range(rows):
        strip = jnp.where(own_src == k, ra_ref[k], strip)
    for j in range(share):
        sb_ref[j] = strip[j : j + 1, :]
    spread_cols(lambda to: sb_ref.at[to], rb_ref.at[c], 2, cols)
    rb_ref[c] = sb_ref[c]

    all_bytes(ru_ref.at[pl.ds(0, rows - 1)], recv_sems.at[1]).wait()
    for g in range(groups):
        part = jnp.zeros((share, LANES), jnp.float32)
        src = lax.shift_right_logical(tile_row[g], 1)
        for k in range(rows):
            part = jnp.where(src == k, ru_ref[k], part)
        upper_ref[pl.ds(r * share, share), g * LANES : (g + 1) * LANES] = part

    all_bytes(rb_ref.at[pl.ds(0, cols - 1)], recv_sems.at[2]).wait()
    for g in range(groups):
        part = jnp.zeros((1, LANES), jnp.float32)
        for k in range(cols):
            part = jnp.where(tile_row[g] == k, rb_ref[k], part)
        row_ref[:, g * LANES : (g + 1) * LANES] = part
    spread_cols(lambda to: row_ref, rc_ref.at[c], 3, cols)
    rc_ref[c] = row_ref[...]

    spread_cols(lambda to: xh_ref.at[pl.ds(to * share, share)], rl_ref.at[c], 4, cols)
    rl_ref[c] = xh_ref[pl.ds(c * share, share), :]
    spread_cols(lambda to: xw_ref.at[pl.ds(to * wchunk, wchunk)], rw_ref.at[c], 5, wowners)

    all_bytes(rc_ref.at[pl.ds(0, cols - 1)], recv_sems.at[3]).wait()
    for j in range(share):
        block_ref[pl.ds(r * share + j, 1), :] = rc_ref[j]
    own_share = pl.ds(r * share, share)
    spread_rows(lambda to: block_ref.at[own_share], block_ref.at[own_share], 6)
    spread_rows(lambda to: upper_ref.at[own_share], upper_ref.at[own_share], 7)

    all_bytes(rl_ref.at[pl.ds(0, cols - 1)], recv_sems.at[4]).wait()
    own_left = pl.ds(c * share, share)
    for g in range(groups):

        def gather_left(k, part):
            return jnp.where(tile_row[g] == k, rl_ref[k], part)

        left_ref[own_left, g * LANES : (g + 1) * LANES] = lax.fori_loop(
            0, cols, gather_left, jnp.zeros((share, LANES), jnp.float32)
        )

    @pl.when(c < wowners)
    def _():
        rw_ref[c] = xw_ref[pl.ds(pl.multiple_of(c * wchunk, wchunk), wchunk), :]
        all_bytes(rw_ref.at[pl.ds(0, cols - 1)], recv_sems.at[5]).wait()
        for g in range(groups):

            def gather_weight(k, part):
                return jnp.where(tile_row[g] == k, rw_ref[k].astype(jnp.float32), part)

            wleft_ref[
                pl.ds(pl.multiple_of(c * wchunk, wchunk), wchunk), g * LANES : (g + 1) * LANES
            ] = lax.fori_loop(0, cols, gather_weight, jnp.zeros((wchunk, LANES), jnp.float32)).astype(
                jnp.bfloat16
            )

    sibling = c + 1 - 2 * lax.rem(c, 2)
    z = c // 2

    def left_copy(slot, size, step, to):
        where = pl.ds(slot * size, size)
        return pltpu.make_async_remote_copy(
            src_ref=left_ref.at[where],
            dst_ref=left_ref.at[where],
            send_sem=ring_send.at[step],
            recv_sem=ring_recv.at[step],
            device_id={"col": to},
            device_id_type=MESH,
        )

    def weight_copy(slot, size, step, to):
        where = pl.ds(pl.multiple_of(slot * size, size), size)
        return pltpu.make_async_remote_copy(
            src_ref=wleft_ref.at[where],
            dst_ref=wleft_ref.at[where],
            send_sem=wring_send.at[step],
            recv_sem=wring_recv.at[step],
            device_id={"col": to},
            device_id_type=MESH,
        )

    wz = wowners // 2
    last = zs - 1
    left_copy(c, share, last, sibling).start()

    @pl.when(z < wz)
    def _():
        weight_copy(c, wchunk, last, sibling).start()

    left_copy(sibling, share, last, sibling).wait_recv()

    @pl.when(z < wz)
    def _():
        weight_copy(sibling, wchunk, last, sibling).wait_recv()

    ways = []
    for s in range(zs // 2):
        ways.append((s, 1, s))
        if s < zs - 1 - zs // 2:
            ways.append((zs // 2 + s, -1, s))

    def z_of(step):
        return lax.rem(z + step + zs, zs)

    for step, way, s in ways:
        to = 2 * z_of(way) + lax.rem(c, 2)
        src = z_of(-way * s)
        if s > 0:
            left_copy(src, 2 * share, step - 1, to).wait_recv()
        left_copy(src, 2 * share, step, to).start()

        @pl.when(src < wz)
        def _():
            if s > 0:
                weight_copy(src, 2 * wchunk, step - 1, to).wait_recv()
            weight_copy(src, 2 * wchunk, step, to).start()

    ends = [(zs // 2 - 1, 1, zs // 2 - 1), (zs - 2, -1, zs - 2 - zs // 2)]
    for step, way, s in ends:
        src = z_of(-way * (s + 1))
        left_copy(src, 2 * share, step, sibling).wait_recv()

        @pl.when(src < wz)
        def _():
            weight_copy(src, 2 * wchunk, step, sibling).wait_recv()

    all_rows = pl.ds(0, (rows - 1) * share)
    all_bytes(block_ref.at[all_rows], recv_sems.at[6]).wait()
    all_bytes(upper_ref.at[all_rows], recv_sems.at[7]).wait()

    all_bytes(ra_ref.at[pl.ds(0, rows - 1)], send_sems.at[0]).wait()
    all_bytes(ru_ref.at[pl.ds(0, rows - 1)], send_sems.at[1]).wait()
    all_bytes(rb_ref.at[pl.ds(0, cols - 1)], send_sems.at[2]).wait()
    all_bytes(rc_ref.at[pl.ds(0, cols - 1)], send_sems.at[3]).wait()
    all_bytes(rl_ref.at[pl.ds(0, cols - 1)], send_sems.at[4]).wait()

    @pl.when(c < wowners)
    def _():
        all_bytes(rw_ref.at[pl.ds(0, wowners - 1)], send_sems.at[5]).wait()

    @pl.when(c >= wowners)
    def _():
        all_bytes(rw_ref.at[pl.ds(0, wowners)], send_sems.at[5]).wait()

    all_bytes(block_ref.at[all_rows], send_sems.at[6]).wait()
    all_bytes(upper_ref.at[all_rows], send_sems.at[7]).wait()
    left_copy(c, share, last, sibling).wait_send()

    @pl.when(z < wz)
    def _():
        weight_copy(c, wchunk, last, sibling).wait_send()

    for step, way, s in ways:
        src = z_of(-way * s)
        left_copy(src, 2 * share, step, sibling).wait_send()

        @pl.when(src < wz)
        def _():
            weight_copy(src, 2 * wchunk, step, sibling).wait_send()


def exchange(hess_inv, weights, removed):
    rows, cols = lax.axis_size("row"), lax.axis_size("col")
    tall, wide = hess_inv.shape
    count = removed.shape[0]
    share = count // rows
    zs = cols // 2
    vmem = pl.BlockSpec(memory_space=pltpu.VMEM)
    f32, bf16 = jnp.float32, jnp.bfloat16
    dma = pltpu.SemaphoreType.DMA
    return pl.pallas_call(
        functools.partial(exchange_kernel, rows, cols),
        out_shape=(
            jax.ShapeDtypeStruct((count, count), f32),
            jax.ShapeDtypeStruct((tall, count), f32),
            jax.ShapeDtypeStruct((wide, count), f32),
            jax.ShapeDtypeStruct((weights.shape[0], count), bf16),
        ),
        in_specs=[vmem] * 4,
        out_specs=(vmem,) * 4,
        scratch_shapes=[
            pltpu.VMEM((wide, LANES), f32),
            pltpu.VMEM((LANES, LANES), f32),
            pltpu.VMEM((tall, LANES), f32),
            pltpu.VMEM((weights.shape[0], LANES), bf16),
            pltpu.VMEM((rows, share, LANES), f32),
            pltpu.VMEM((rows, share, LANES), f32),
            pltpu.VMEM((share, 1, LANES), f32),
            pltpu.VMEM((cols, 1, LANES), f32),
            pltpu.VMEM((1, count), f32),
            pltpu.VMEM((cols, 1, count), f32),
            pltpu.VMEM((cols, share, LANES), f32),
            pltpu.VMEM((cols, 16, LANES), bf16),
            dma((8,)),
            dma((8,)),
            dma((zs,)),
            dma((zs,)),
            dma((zs,)),
            dma((zs,)),
        ],
        compiler_params=pltpu.CompilerParams(
            collective_id=0, has_side_effects=True, vmem_limit_bytes=48 * 1024 * 1024
        ),
        cost_estimate=pl.CostEstimate(
            flops=2 * tall * wide * LANES * 6, bytes_accessed=8 * 1024 * 1024, transcendentals=0
        ),
        name="exchange",
    )(hess_inv, weights, removed.reshape(count // LANES, LANES), removed.reshape(count, 1))


def on_device(hess_inv, weights, removed):
    block, left, upper, weight_left = exchange(hess_inv, weights, removed)
    factor = jnp.linalg.cholesky(block)
    identity = jnp.eye(block.shape[0], dtype=jnp.float32)
    factor_inv = jax.scipy.linalg.solve_triangular(factor, identity, lower=True)
    block_inv = jnp.dot(factor_inv.T, factor_inv, precision=HIGHEST)
    coupling = jnp.dot(block_inv, upper.T, precision=HIGHEST)
    hess_out = hess_inv - jnp.dot(left, coupling, precision=HIGHEST)
    weight_fix = jnp.dot(weight_left.astype(jnp.float32), coupling, precision=HIGHEST)
    weight_out = (weights.astype(jnp.float32) - weight_fix).astype(jnp.bfloat16)
    return (hess_out, weight_out)


def solution(mesh):
    placed = (P("row", "col"), P("row", "col"), P())
    return jax.shard_map(
        on_device,
        mesh=mesh,
        in_specs=placed,
        out_specs=(P("row", "col"), P("row", "col")),
        check_vma=False,
    )
```

time: 817 us -> 298 us (0.36)
  the two profiles are of different devices: /device:TPU:24 before, /device:TPU:2 now
where the time goes in v1:
time: 298 us; the launch traced here: 293 us
  other arithmetic  133 us (45%)
  Pallas kernels  110 us (37%)
  matrix products  23.9 us (8%)
  local copies, waits for them, and re-layouts  23.2 us (8%)
  between operations  3.72 us (1%)
    pallas_call x1, Pallas kernels, exchange(): pl.pallas_call(functools.partial(exchange_kernel, rows, cols), out_shape=...  110 us
    another operation x14, other arithmetic, on_device(): factor = jnp.linalg.cholesky(block)  90.4 us
    another operation x3, other arithmetic, on_device(): factor_inv = jax.scipy.linalg.solve_triangular(factor, identity, lower=True)  40.4 us
    another operation x12, local copies, waits for them, and re-layouts  11.6 us
    another operation x6, matrix products, on_device(): factor = jnp.linalg.cholesky(block)  7.88 us
    unnamed x22, local copies, waits for them, and re-layouts  6.5 us

profile of v1, /device:TPU:2, one launch (start us, length us, event | category | flops | bytes accessed | tf_op | source)
XLA Modules:
  0.0 293.4 jit_solution(6385684244417821591)
XLA Ops:
  0.6 1.5 copy.6.rem_col_ref
  2.2 1.0 copy-done.2
  3.2 0.9 copy-done.4
  4.1 0.7 copy-done.5
  4.8 110.1 %exchange.1 = (f32[512,512]{1,0:T(8,128)S(1)}, f32[1024,512]{1,0:T(8,128)S(1)}, f32[512,512]{1,0:T(8,128)S(1)}, bf16[384,512]{1,0:T(8,128)(2,1)S(1)}) custom-call(f32[1024,512]{1,0:T(8,128)} %hess_ref.1, bf16[384,512]{1,0:T(8,128)(2,1)S(1)} %copy-done.2, s32[4,128]{1,0:T(4,128)S(1)} %bitcast.57, s32[512,1]{1,0:T(8,128)S(1)} %copy-done.4), custom_call_target="tpu_custom_call" | custom-call | flops 805306368 | bytes 8388608 | tf_op jit(solution)/shard_map/exchange/pallas_call | solution.py:313
  114.9 1.0 copy-done
  115.8 1.3 copy.7
  117.2 1.4 fusion.9
  118.6 0.0 copy-start.6
  118.6 1.0 copy-done.6
  119.6 11.7 %cholesky.104 = f32[128,128]{1,0:T(8,128)S(1)} custom-call(f32[128,128]{1,0:T(8,128)S(1)} %cholesky.266), custom_call_target="Cholesky" | custom-call | tf_op jit(solution)/shard_map/jit(cholesky)/cholesky | solution.py:355
  131.3 0.6 copy-done.10
  131.9 10.4 %custom-call.31 = f32[1,128,128]{1,2,0:T(8,128)} custom-call(f32[1,128,128]{2,1,0:T(8,128)S(1)} %get-tuple-element.37), custom_call_target="InvertDiagBlocksLowerTriangular" | custom-call | tf_op jit(solution)/shard_map/jit(cholesky)/cholesky | solution.py:355
  142.4 1.0 cholesky.224
  143.3 1.2 constant_dynamic-update-slice_fusion.3
  144.6 1.3 convolution_subtract_fusion.5
  145.8 0.0 copy-start.8
  145.9 0.7 copy-done.8
  146.5 0.6 cholesky.270
  147.1 13.2 %cholesky.217 = f32[128,128]{1,0:T(8,128)} custom-call(f32[128,128]{1,0:T(8,128)} %cholesky.270), custom_call_target="Cholesky" | custom-call | tf_op jit(solution)/shard_map/jit(cholesky)/cholesky | solution.py:355
  160.3 1.5 select_reduce_fusion.2
  161.8 0.7 compare_reduce_fusion.2
  163.8 11.4 %custom-call.32 = f32[1,128,128]{1,2,0:T(8,128)} custom-call(f32[1,128,128]{2,1,0:T(8,128)} %get-tuple-element.34), custom_call_target="InvertDiagBlocksLowerTriangular" | custom-call | tf_op jit(solution)/shard_map/jit(cholesky)/cholesky | solution.py:355
  175.2 1.2 convolution_dynamic-update-slice_fusion
  176.3 1.3 convolution_subtract_fusion.6
  177.6 0.6 copy-done.9
  178.3 0.6 cholesky.275
  178.9 13.2 %cholesky.238 = f32[128,128]{1,0:T(8,128)} custom-call(f32[128,128]{1,0:T(8,128)} %cholesky.275), custom_call_target="Cholesky" | custom-call | tf_op jit(solution)/shard_map/jit(cholesky)/cholesky | solution.py:355
  192.1 1.5 select_reduce_fusion.1
  193.6 0.7 compare_reduce_fusion.1
  195.0 11.3 %custom-call.33 = f32[1,128,128]{1,2,0:T(8,128)} custom-call(f32[1,128,128]{2,1,0:T(8,128)} %get-tuple-element.31), custom_call_target="InvertDiagBlocksLowerTriangular" | custom-call | tf_op jit(solution)/shard_map/jit(cholesky)/cholesky | solution.py:355
  206.2 1.1 convolution_dynamic-update-slice_fusion.1
  207.3 1.9 convolution_subtract_fusion.7
  209.2 13.4 %cholesky.255 = f32[128,128]{1,0:T(8,128)} custom-call(f32[128,128]{1,0:T(8,128)} %convolution_subtract_fusion.7), custom_call_target="Cholesky" | custom-call | tf_op jit(solution)/shard_map/jit(cholesky)/cholesky | solution.py:355
  222.5 0.9 select_reduce_fusion
  223.4 0.6 compare_reduce_fusion
  224.7 1.1 select_select_fusion
  225.8 11.7 %while.1 = (s32[]{:T(128)}, f32[512,512]{1,0:T(8,128)}, s32[4,2]{0,1:T(2,128)S(1)}, f32[4,128,128]{2,1,0:T(8,128)S(1)}, s32[]{:T(128)}) while((s32[]{:T(128)}, f32[512,512]{1,0:T(8,128)}, s32[4,2]{0,1:T(2,128)S(1)}, f32[4,128,128]{2,1,0:T(8,128)S(1)}, s32[]{:T(128)}) %tuple.31), condition=%wide.while_cond, body=%wide.while_body.sunk | while | flops 2 | bytes 131181 | solution.py:357
  225.8 0.1 constant_dynamic-slice_fusion.2
  225.9 0.6 fusion.55
  226.5 2.3 bitcast_dynamic-update-slice_fusion.2
  228.8 0.1 constant_dynamic-slice_fusion.2
  228.8 0.6 fusion.55
  229.4 2.3 bitcast_dynamic-update-slice_fusion.2
  231.7 0.1 constant_dynamic-slice_fusion.2
  231.8 0.6 fusion.55
  232.4 2.3 bitcast_dynamic-update-slice_fusion.2
  234.6 0.1 constant_dynamic-slice_fusion.2
  234.7 0.6 fusion.55
  235.3 2.2 bitcast_dynamic-update-slice_fusion.2
  237.5 39.3 %custom-call.34 = f32[4,128,128]{1,2,0:T(8,128)S(1)} custom-call(f32[4,128,128]{2,1,0:T(8,128)S(1)} %get-tuple-element.17), custom_call_target="InvertDiagBlocksLowerTriangular" | custom-call | tf_op jit(solution)/shard_map/jit(_solve_triangular)/triangular_solve | solution.py:357
  276.8 0.1 iota_compare_fusion
  276.9 0.3 fusion.20
  277.3 0.1 fusion.18
  277.4 1.2 convolution_subtract_fusion.3
  278.6 0.4 fusion.32
  279.0 1.3 convolution_subtract_fusion.2
  280.4 0.4 fusion.30
  280.8 1.6 convolution_subtract_fusion.4
  282.4 0.4 fusion.29
  282.9 1.9 fusion.1
  284.8 1.9 fusion.42
  286.7 1.6 fusion
  288.3 4.8 %convolution_subtract_fusion = f32[1024,512]{1,0:T(8,128)} fusion(f32[1024,512]{1,0:T(8,128)S(1)} %copy-done.7, f32[1024,512]{1,0:T(8,128)S(1)} %get-tuple-element.6, f32[512,512]{1,0:T(8,128)S(1)} %fusion.42), kind=kOutput, calls=%fused_computation.2 | convolution fusion | flops 3221749760 | bytes 7340032 | tf_op jit(solution)/shard_map/dot_general | solution.py:360
  (17 shorter events, 0.1 us)
Async XLA Ops:
  2.2 1.0 copy-start.2
  3.2 0.9 copy-start.4
  4.1 0.7 copy-start.5
  114.9 1.0 copy-start
  118.6 1.0 copy-start.6
  131.3 0.6 copy-start.10
  145.8 0.7 copy-start.8
  177.6 0.7 copy-start.9
  280.8 4.0 %copy-start.1 = (f32[512,512]{1,0:T(8,128)S(1)}, f32[512,512]{1,0:T(8,128)}, u32[]{:S(2)}) copy-start(f32[512,512]{1,0:T(8,128)} %copy-done) | copy-start | bytes 3145732
  284.8 1.9 copy-start.3
  284.8 3.5 %copy-start.7 = (f32[1024,512]{1,0:T(8,128)S(1)}, f32[1024,512]{1,0:T(8,128)}, u32[]{:S(2)}) copy-start(f32[1024,512]{1,0:T(8,128)} %hess_ref.1) | copy-start | bytes 6291460

commit v2 on v1

--- a/solution.py
+++ b/solution.py
@@ -14,6 +14,85 @@
 
 def all_bytes(ref, sem):
     return pltpu.make_async_copy(ref, ref, sem)
+
+
+def split3(x):
+    high = x.astype(jnp.bfloat16)
+    rest = x - high.astype(jnp.float32)
+    mid = rest.astype(jnp.bfloat16)
+    return high, mid, (rest - mid.astype(jnp.float32)).astype(jnp.bfloat16)
+
+
+def dot6(a, b, b_dim=0):
+    ah, am, al = split3(a)
+    bh, bm, bl = split3(b)
+    return lax.dot_general(
+        jnp.concatenate([ah, al, am, am, ah, ah], axis=1),
+        jnp.concatenate([bl, bh, bm, bh, bm, bh], axis=b_dim),
+        (((1,), (b_dim,)), ((), ())),
+        preferred_element_type=jnp.float32,
+    )
+
+
+def eliminate(columns, panel):
+    count = len(columns)
+    sub = lax.broadcasted_iota(jnp.int32, (8, LANES), 0)
+
+    def row(x, j):
+        return jnp.broadcast_to(x[j // 8][j % 8 : j % 8 + 1, :], (8, LANES))
+
+    todo = [list(x) for x in columns] + [list(panel)]
+    for j in range(count):
+        pivot = todo.pop(0)
+        scale = 1.0 / row(pivot, j)
+        for x in todo:
+            new = row(x, j) * scale
+            for t in range(len(x)):
+                x[t] = x[t] - pivot[t] * new
+            x[j // 8] = jnp.where(sub == j % 8, new, x[j // 8])
+    return todo[0]
+
+
+def invert_tile(tile):
+    count = tile.shape[0] // 8
+    v = [tile[8 * i : 8 * i + 8, :] for i in range(count)]
+    lane = lax.broadcasted_iota(jnp.int32, (8, LANES), 1)
+    sub = lax.broadcasted_iota(jnp.int32, (8, LANES), 0)
+
+    def column(x, k):
+        return jnp.broadcast_to(x[:, k : k + 1], (8, LANES))
+
+    for b in range(count // 2):
+        k = 16 * b
+        rows = [2 * b, 2 * b + 1]
+        ahead = [i for i in (2 * b + 2, 2 * b + 3) if i < count]
+        rest = [i for i in range(count) if i not in rows and i not in ahead]
+        inside = (lane >= k) & (lane < k + 16)
+        columns = [[column(v[i], k + q) for i in rows] for q in range(16)]
+        panel = [jnp.where(inside, jnp.where(lane == sub + 8 * i, 1.0, 0.0), v[i]) for i in rows]
+        new = eliminate(columns, panel)
+        w = list(v)
+        for i in ahead:
+            terms = [
+                column(v[i], k + q)
+                * jnp.broadcast_to(new[q // 8][q % 8 : q % 8 + 1, :], (8, LANES))
+                for q in range(16)
+            ]
+            while len(terms) > 1:
+                terms = [terms[z] + terms[z + 1] for z in range(0, len(terms), 2)]
+            w[i] = jnp.where(inside, 0.0, v[i]) - terms[0]
+        for t, i in enumerate(rows):
+            w[i] = new[t]
+        change = jnp.dot(
+            jnp.concatenate([v[i] for i in rest], axis=0)[:, k : k + 16],
+            jnp.concatenate(new, axis=0),
+            precision=HIGHEST,
+            preferred_element_type=jnp.float32,
+        )
+        for z, i in enumerate(rest):
+            w[i] = jnp.where(inside, 0.0, v[i]) - change[8 * z : 8 * z + 8]
+        v = w
+    return jnp.concatenate(v, axis=0)
 
 
 def exchange_kernel(
@@ -23,10 +102,12 @@
     weight_ref,
     rem_row_ref,
     rem_col_ref,
+    coupling_ref,
+    left_ref,
+    wleft_ref,
     block_ref,
-    left_ref,
     upper_ref,
-    wleft_ref,
+    strip_ref,
     yt_ref,
     bp_ref,
     xh_ref,
@@ -123,9 +204,20 @@
     spread_rows(lambda to: yt_ref.at[pl.ds(to * share, share)], ru_ref.at[r], 1)
     ru_ref[r] = yt_ref[pl.ds(r * share, share), :]
 
-    xh_ref[...] = jnp.dot(
-        hess_ref[...], pick_col, precision=HIGHEST, preferred_element_type=jnp.float32
+    half = LANES // 2
+    low = lax.broadcasted_iota(jnp.int32, (wide, LANES), 1) < half
+    fold = pick_col + pltpu.roll(pick_col, half, 1)
+    pick_half = jnp.concatenate(
+        [jnp.where(low, fold, 0.0), jnp.where(low, 0.0, fold)], axis=0
+    ).astype(jnp.bfloat16)
+    parts = hess_ref[...].reshape(tall // share, 2, share // 2, wide)
+    pairs = jnp.concatenate(
+        [parts[:, 0].reshape(tall // 2, wide), parts[:, 1].reshape(tall // 2, wide)], axis=1
     )
+    packed = [
+        jnp.dot(x, pick_half, preferred_element_type=jnp.float32) for x in split3(pairs)
+    ]
+    xh_ref[...] = (packed[2] + packed[1]) + packed[0]
     xw_ref[...] = jnp.dot(
         weight_ref[...], pick_col.astype(jnp.bfloat16), preferred_element_type=jnp.float32
     ).astype(jnp.bfloat16)
@@ -159,8 +251,8 @@
     spread_cols(lambda to: row_ref, rc_ref.at[c], 3, cols)
     rc_ref[c] = row_ref[...]
 
-    spread_cols(lambda to: xh_ref.at[pl.ds(to * share, share)], rl_ref.at[c], 4, cols)
-    rl_ref[c] = xh_ref[pl.ds(c * share, share), :]
+    spread_cols(lambda to: xh_ref.at[pl.ds(to * (share // 2), share // 2)], rl_ref.at[c], 4, cols)
+    rl_ref[c] = xh_ref[pl.ds(c * (share // 2), share // 2), :]
     spread_cols(lambda to: xw_ref.at[pl.ds(to * wchunk, wchunk)], rw_ref.at[c], 5, wowners)
 
     all_bytes(rc_ref.at[pl.ds(0, cols - 1)], recv_sems.at[3]).wait()
@@ -171,14 +263,25 @@
     spread_rows(lambda to: upper_ref.at[own_share], upper_ref.at[own_share], 7)
 
     all_bytes(rl_ref.at[pl.ds(0, cols - 1)], recv_sems.at[4]).wait()
-    own_left = pl.ds(c * share, share)
+    first = lax.broadcasted_iota(jnp.int32, (share // 2, LANES), 1) < half
     for g in range(groups):
-
-        def gather_left(k, part):
-            return jnp.where(tile_row[g] == k, rl_ref[k], part)
-
-        left_ref[own_left, g * LANES : (g + 1) * LANES] = lax.fori_loop(
-            0, cols, gather_left, jnp.zeros((share, LANES), jnp.float32)
+        turned = pltpu.roll(jnp.broadcast_to(tile_row[g], (8, LANES)), half, 1)[0:1, :]
+
+        def gather_left(k, carry):
+            straight, cross = carry
+            x = rl_ref[k]
+            return (
+                jnp.where(tile_row[g] == k, x, straight),
+                jnp.where(turned == k, x, cross),
+            )
+
+        zero = jnp.zeros((share // 2, LANES), jnp.float32)
+        straight, cross = lax.fori_loop(0, cols, gather_left, (zero, zero))
+        cross = pltpu.roll(cross, half, 1)
+        where = slice(g * LANES, (g + 1) * LANES)
+        left_ref[pl.ds(c * share, share // 2), where] = jnp.where(first, straight, cross)
+        left_ref[pl.ds(c * share + share // 2, share // 2), where] = jnp.where(
+            first, cross, straight
         )
 
     @pl.when(c < wowners)
@@ -197,78 +300,144 @@
             )
 
     sibling = c + 1 - 2 * lax.rem(c, 2)
+    parity = lax.rem(c, 2)
     z = c // 2
-
-    def left_copy(slot, size, step, to):
-        where = pl.ds(slot * size, size)
-        return pltpu.make_async_remote_copy(
-            src_ref=left_ref.at[where],
-            dst_ref=left_ref.at[where],
-            send_sem=ring_send.at[step],
-            recv_sem=ring_recv.at[step],
-            device_id={"col": to},
-            device_id_type=MESH,
+    wz = wowners // 2
+    plus, minus = zs // 2, zs - 1 - zs // 2
+    sib_plus, sib_minus = 2, 3
+    away = lax.rem(z + 1, zs), lax.rem(z + zs - 1, zs)
+
+    bases = (0, plus, plus + minus, plus + minus + sib_plus, zs + sib_plus + sib_minus - 1)
+    bases += (bases[4] + plus - sib_plus + 1 - sib_minus - 1,)
+
+    def shares(z_src, side, kind, step, to, go):
+        slot = 2 * z_src + side
+        at = pl.ds(slot * share, share)
+        at_sem = bases[kind] + (jnp.maximum(step - sib_plus, 0) if kind == 4 else step)
+        go(
+            pltpu.make_async_remote_copy(
+                src_ref=left_ref.at[at],
+                dst_ref=left_ref.at[at],
+                send_sem=ring_send.at[at_sem],
+                recv_sem=ring_recv.at[at_sem],
+                device_id={"col": to},
+                device_id_type=MESH,
+            )
         )
 
-    def weight_copy(slot, size, step, to):
-        where = pl.ds(pl.multiple_of(slot * size, size), size)
-        return pltpu.make_async_remote_copy(
-            src_ref=wleft_ref.at[where],
-            dst_ref=wleft_ref.at[where],
-            send_sem=wring_send.at[step],
-            recv_sem=wring_recv.at[step],
-            device_id={"col": to},
-            device_id_type=MESH,
-        )
-
-    wz = wowners // 2
-    last = zs - 1
-    left_copy(c, share, last, sibling).start()
-
-    @pl.when(z < wz)
-    def _():
-        weight_copy(c, wchunk, last, sibling).start()
-
-    left_copy(sibling, share, last, sibling).wait_recv()
-
-    @pl.when(z < wz)
-    def _():
-        weight_copy(sibling, wchunk, last, sibling).wait_recv()
-
-    ways = []
-    for s in range(zs // 2):
-        ways.append((s, 1, s))
-        if s < zs - 1 - zs // 2:
-            ways.append((zs // 2 + s, -1, s))
-
-    def z_of(step):
-        return lax.rem(z + step + zs, zs)
-
-    for step, way, s in ways:
-        to = 2 * z_of(way) + lax.rem(c, 2)
-        src = z_of(-way * s)
-        if s > 0:
-            left_copy(src, 2 * share, step - 1, to).wait_recv()
-        left_copy(src, 2 * share, step, to).start()
-
-        @pl.when(src < wz)
-        def _():
-            if s > 0:
-                weight_copy(src, 2 * wchunk, step - 1, to).wait_recv()
-            weight_copy(src, 2 * wchunk, step, to).start()
-
-    ends = [(zs // 2 - 1, 1, zs // 2 - 1), (zs - 2, -1, zs - 2 - zs // 2)]
-    for step, way, s in ends:
-        src = z_of(-way * (s + 1))
-        left_copy(src, 2 * share, step, sibling).wait_recv()
-
-        @pl.when(src < wz)
-        def _():
-            weight_copy(src, 2 * wchunk, step, sibling).wait_recv()
+        @pl.when(z_src < wz)
+        def _():
+            wat = pl.ds(pl.multiple_of(slot * wchunk, wchunk), wchunk)
+            go(
+                pltpu.make_async_remote_copy(
+                    src_ref=wleft_ref.at[wat],
+                    dst_ref=wleft_ref.at[wat],
+                    send_sem=wring_send.at[at_sem],
+                    recv_sem=wring_recv.at[at_sem],
+                    device_id={"col": to},
+                    device_id_type=MESH,
+                )
+            )
+
+    start, recv, sent = (lambda d: d.start()), (lambda d: d.wait_recv()), (lambda d: d.wait_send())
+
+    def behind(s):
+        return lax.rem(z + zs - s, zs)
+
+    def before(s):
+        return lax.rem(z + s, zs)
+
+    def send_own(s, go):
+        @pl.when(s < plus)
+        def _():
+            shares(behind(s), parity, 0, s, 2 * away[0] + parity, go)
+
+        @pl.when(s < minus)
+        def _():
+            shares(before(s), parity, 1, s, 2 * away[1] + parity, go)
+
+        @pl.when((s == 0) | ((s > sib_plus) & (s <= plus)))
+        def _():
+            shares(behind(s), parity, 4, s, sibling, go)
+
+        @pl.when((s > sib_minus) & (s <= minus))
+        def _():
+            shares(before(s), parity, 5, s, sibling, go)
+
+    def send_other(s, go):
+        @pl.when(s < sib_plus)
+        def _():
+            shares(behind(s), 1 - parity, 2, s, 2 * away[0] + parity, go)
+
+        @pl.when(s < sib_minus)
+        def _():
+            shares(before(s), 1 - parity, 3, s, 2 * away[1] + parity, go)
+
+    def ring_begin():
+        send_own(0, start)
+        shares(z, 1 - parity, 4, 0, sibling, recv)
+        send_other(0, start)
+
+    def ring_step(s):
+        @pl.when(s <= plus)
+        def _():
+            shares(behind(s), parity, 0, s - 1, sibling, recv)
+
+        @pl.when(s <= minus)
+        def _():
+            shares(before(s), parity, 1, s - 1, sibling, recv)
+
+        send_own(s, start)
+
+        @pl.when(s <= sib_plus)
+        def _():
+            shares(behind(s), 1 - parity, 2, s - 1, sibling, recv)
+
+        @pl.when(s <= sib_minus)
+        def _():
+            shares(before(s), 1 - parity, 3, s - 1, sibling, recv)
+
+        send_other(s, start)
+
+    def ring_end():
+        @pl.loop(sib_plus + 1, plus + 1)
+        def _(s):
+            shares(behind(s), 1 - parity, 4, s, sibling, recv)
+
+            @pl.when((s > sib_minus) & (s <= minus))
+            def _():
+                shares(before(s), 1 - parity, 5, s, sibling, recv)
+
+    def ring_sent():
+        @pl.loop(0, plus + 1)
+        def _(s):
+            send_own(s, sent)
+            send_other(s, sent)
+
+    ring_begin()
 
     all_rows = pl.ds(0, (rows - 1) * share)
     all_bytes(block_ref.at[all_rows], recv_sems.at[6]).wait()
+    all_bytes(block_ref.at[all_rows], send_sems.at[6]).wait()
+
+    def invert_step(k, carry):
+        at = pl.ds(pl.multiple_of(k * LANES, LANES), LANES)
+        inverse = invert_tile(block_ref[at, at])
+        ring_step(2 * k + 1)
+        strip_ref[...] = dot6(inverse, block_ref[at, :])
+        strip_ref[:, at] = inverse
+        column = block_ref[:, at]
+        block_ref[:, at] = jnp.zeros((count, LANES), jnp.float32)
+        block_ref[...] -= dot6(column, strip_ref[...])
+        block_ref[at, :] = strip_ref[...]
+        ring_step(2 * k + 2)
+        return carry
+
+    lax.fori_loop(0, groups, invert_step, 0)
+
     all_bytes(upper_ref.at[all_rows], recv_sems.at[7]).wait()
+    coupling_ref[...] = dot6(block_ref[...], upper_ref[...], b_dim=1)
+    ring_end()
 
     all_bytes(ra_ref.at[pl.ds(0, rows - 1)], send_sems.at[0]).wait()
     all_bytes(ru_ref.at[pl.ds(0, rows - 1)], send_sems.at[1]).wait()
@@ -284,21 +453,8 @@
     def _():
         all_bytes(rw_ref.at[pl.ds(0, wowners)], send_sems.at[5]).wait()
 
-    all_bytes(block_ref.at[all_rows], send_sems.at[6]).wait()
     all_bytes(upper_ref.at[all_rows], send_sems.at[7]).wait()
-    left_copy(c, share, last, sibling).wait_send()
-
-    @pl.when(z < wz)
-    def _():
-        weight_copy(c, wchunk, last, sibling).wait_send()
-
-    for step, way, s in ways:
-        src = z_of(-way * s)
-        left_copy(src, 2 * share, step, sibling).wait_send()
-
-        @pl.when(src < wz)
-        def _():
-            weight_copy(src, 2 * wchunk, step, sibling).wait_send()
+    ring_sent()
 
 
 def exchange(hess_inv, weights, removed):
@@ -313,17 +469,19 @@
     return pl.pallas_call(
         functools.partial(exchange_kernel, rows, cols),
         out_shape=(
-            jax.ShapeDtypeStruct((count, count), f32),
+            jax.ShapeDtypeStruct((count, wide), f32),
             jax.ShapeDtypeStruct((tall, count), f32),
-            jax.ShapeDtypeStruct((wide, count), f32),
             jax.ShapeDtypeStruct((weights.shape[0], count), bf16),
         ),
         in_specs=[vmem] * 4,
-        out_specs=(vmem,) * 4,
+        out_specs=(vmem,) * 3,
         scratch_shapes=[
+            pltpu.VMEM((count, count), f32),
+            pltpu.VMEM((wide, count), f32),
+            pltpu.VMEM((LANES, count), f32),
             pltpu.VMEM((wide, LANES), f32),
             pltpu.VMEM((LANES, LANES), f32),
-            pltpu.VMEM((tall, LANES), f32),
+            pltpu.VMEM((tall // 2, LANES), f32),
             pltpu.VMEM((weights.shape[0], LANES), bf16),
             pltpu.VMEM((rows, share, LANES), f32),
             pltpu.VMEM((rows, share, LANES), f32),
@@ -331,14 +489,14 @@
             pltpu.VMEM((cols, 1, LANES), f32),
             pltpu.VMEM((1, count), f32),
             pltpu.VMEM((cols, 1, count), f32),
-            pltpu.VMEM((cols, share, LANES), f32),
+            pltpu.VMEM((cols, share // 2, LANES), f32),
             pltpu.VMEM((cols, 16, LANES), bf16),
             dma((8,)),
             dma((8,)),
-            dma((zs,)),
-            dma((zs,)),
-            dma((zs,)),
-            dma((zs,)),
+            dma((2 * zs,)),
+            dma((2 * zs,)),
+            dma((2 * zs,)),
+            dma((2 * zs,)),
         ],
         compiler_params=pltpu.CompilerParams(
             collective_id=0, has_side_effects=True, vmem_limit_bytes=48 * 1024 * 1024
@@ -351,12 +509,7 @@
 
 
 def on_device(hess_inv, weights, removed):
-    block, left, upper, weight_left = exchange(hess_inv, weights, removed)
-    factor = jnp.linalg.cholesky(block)
-    identity = jnp.eye(block.shape[0], dtype=jnp.float32)
-    factor_inv = jax.scipy.linalg.solve_triangular(factor, identity, lower=True)
-    block_inv = jnp.dot(factor_inv.T, factor_inv, precision=HIGHEST)
-    coupling = jnp.dot(block_inv, upper.T, precision=HIGHEST)
+    coupling, left, weight_left = exchange(hess_inv, weights, removed)
     hess_out = hess_inv - jnp.dot(left, coupling, precision=HIGHEST)
     weight_fix = jnp.dot(weight_left.astype(jnp.float32), coupling, precision=HIGHEST)
     weight_out = (weights.astype(jnp.float32) - weight_fix).astype(jnp.bfloat16)

time: 298 us -> 117 us (0.39); the launches traced: 293 us -> 117 us
  other arithmetic: 133 us -> 0 us
  local copies, waits for them, and re-layouts: 23.2 us -> 2.5 us
  matrix products: 23.9 us -> 6.48 us
  between operations: 3.72 us -> 0.66 us
  Pallas kernels: 110 us -> 107 us
    another operation x17 -> x0, other arithmetic: 131 us -> none  [the longest x14 90.4 us: on_device(): factor = jnp.linalg.cholesky(block)]
    another operation x17 -> x0, local copies, waits for them, and re-layouts: 13.8 us -> none
    another operation x13 -> x0, matrix products: 13.6 us -> none  [the longest x6 7.88 us: on_device(): factor = jnp.linalg.cholesky(block)]
    unnamed x22 -> x6, local copies, waits for them, and re-layouts: 6.5 us -> 1.68 us
    dot_general x2 -> x0, matrix products: 3.79 us -> none  [the longest x1 1.92 us: on_device(): block_inv = jnp.dot(factor_inv.T, factor_inv, precision=HIGHEST)]
    pallas_call x1, Pallas kernels: 110 us -> 107 us  [exchange(): pl.pallas_call(functools.partial(exchange_kernel, rows, cols), out_shape=...]
where the time goes in v2:
time: 117 us
  Pallas kernels  107 us (91%)
  matrix products  6.48 us (6%)
  local copies, waits for them, and re-layouts  2.5 us (2%)
    pallas_call x1, Pallas kernels, exchange(): pl.pallas_call(functools.partial(exchange_kernel, rows, cols), out_shape=...  107 us
    dot_general x1, matrix products, on_device(): hess_out = hess_inv - jnp.dot(left, coupling, precision=HIGHEST)  4.87 us

profile of v2, /device:TPU:2, one launch (start us, length us, event | category | flops | bytes accessed | tf_op | source)
XLA Modules:
  0.0 116.5 jit_solution(840293869563423372)
XLA Ops:
  0.6 0.8 copy.5.rem_col_ref
  1.5 0.0 copy-start
  1.5 1.0 copy-done
  2.5 0.0 copy-start.1
  2.5 0.7 copy-done.1
  3.1 0.0 copy-start.2
  3.1 106.9 %exchange.1 = (f32[512,512]{1,0:T(8,128)S(1)}, f32[1024,512]{1,0:T(8,128)S(1)}, bf16[384,512]{1,0:T(8,128)(2,1)S(1)}) custom-call(f32[1024,512]{1,0:T(8,128)} %hess_ref.1, bf16[384,512]{1,0:T(8,128)(2,1)S(1)} %copy-done, s32[4,128]{1,0:T(4,128)S(1)} %bitcast.7, s32[512,1]{1,0:T(8,128)S(1)} %copy.5.rem_col_ref), custom_call_target="tpu_custom_call" | custom-call | flops 805306368 | bytes 8388608 | tf_op jit(solution)/shard_map/exchange/pallas_call | solution.py:469
  110.0 0.0 copy-done.2
  110.0 4.9 %convolution_subtract_fusion = f32[1024,512]{1,0:T(8,128)} fusion(f32[1024,512]{1,0:T(8,128)S(1)} %copy-done.2, f32[1024,512]{1,0:T(8,128)S(1)} %get-tuple-element.5, f32[512,512]{1,0:T(8,128)S(1)} %get-tuple-element.6), kind=kOutput, calls=%fused_computation | convolution fusion | flops 3221749760 | bytes 7340032 | tf_op jit(solution)/shard_map/dot_general | solution.py:513
  114.9 1.6 %fusion = bf16[384,512]{1,0:T(8,128)(2,1)} fusion(bf16[384,512]{1,0:T(8,128)(2,1)S(1)} %get-tuple-element.7, f32[512,512]{1,0:T(8,128)S(1)} %get-tuple-element.6, bf16[384,512]{1,0:T(8,128)(2,1)S(1)} %copy-done), kind=kOutput, calls=%fused_computation.2 | convolution fusion | flops 1208549376 | bytes 2228224 | tf_op jit(solution)/shard_map/dot_general | solution.py:514
Async XLA Ops:
  1.5 1.0 copy-start
  2.5 0.7 copy-start.1
  3.1 106.9 %copy-start.2 = (f32[1024,512]{1,0:T(8,128)S(1)}, f32[1024,512]{1,0:T(8,128)}, u32[]{:S(2)}) copy-start(f32[1024,512]{1,0:T(8,128)} %hess_ref.1) | copy-start | bytes 6291460

commit v3 on v2

--- a/solution.py
+++ b/solution.py
@@ -98,13 +98,16 @@
 def exchange_kernel(
     rows,
     cols,
-    hess_ref,
-    weight_ref,
+    hess_hbm,
+    weight_hbm,
     rem_row_ref,
-    rem_col_ref,
     coupling_ref,
     left_ref,
     wleft_ref,
+    hess_ref,
+    weight_ref,
+    rem_col_ref,
+    load_sems,
     block_ref,
     upper_ref,
     strip_ref,
@@ -137,6 +140,12 @@
     wchunk = 16
     wowners = weight_ref.shape[0] // wchunk
 
+    loads = [
+        pltpu.make_async_copy(hess_hbm, hess_ref, load_sems.at[0]),
+        pltpu.make_async_copy(weight_hbm, weight_ref, load_sems.at[1]),
+    ]
+    for load in loads:
+        load.start()
     barrier = pltpu.get_barrier_semaphore()
 
     @pl.loop(1, rows)
@@ -150,6 +159,11 @@
         pl.semaphore_signal(
             barrier, inc=1, device_id={"col": lax.rem(c + k, cols)}, device_id_type=MESH
         )
+
+    for g in range(groups):
+        rem_col_ref[g * LANES : (g + 1) * LANES, :] = jnp.broadcast_to(
+            rem_row_ref[g : g + 1, :], (LANES, LANES)
+        ).T
 
     col_iota = lax.broadcasted_iota(jnp.int32, (wide, LANES), 0) + c * wide
     row_iota = lax.broadcasted_iota(jnp.int32, (LANES, tall), 1) + r * tall
@@ -158,9 +172,11 @@
     for g in range(groups):
         pick_col = jnp.where(rem_row_ref[g : g + 1, :] == col_iota, 1.0, pick_col)
         pick_row = jnp.where(
-            rem_col_ref[g * LANES : (g + 1) * LANES, :] == row_iota, 1.0, pick_row
+            rem_col_ref[g * LANES : (g + 1) * LANES, 0:1] == row_iota, 1.0, pick_row
         )
 
+    for load in loads:
+        load.wait()
     own_rows = jnp.dot(
         pick_row, hess_ref[...], precision=HIGHEST, preferred_element_type=jnp.float32
     )
@@ -242,6 +258,9 @@
             part = jnp.where(src == k, ru_ref[k], part)
         upper_ref[pl.ds(r * share, share), g * LANES : (g + 1) * LANES] = part
 
+    own_share = pl.ds(r * share, share)
+    spread_rows(lambda to: upper_ref.at[own_share], upper_ref.at[own_share], 7)
+
     all_bytes(rb_ref.at[pl.ds(0, cols - 1)], recv_sems.at[2]).wait()
     for g in range(groups):
         part = jnp.zeros((1, LANES), jnp.float32)
@@ -258,9 +277,7 @@
     all_bytes(rc_ref.at[pl.ds(0, cols - 1)], recv_sems.at[3]).wait()
     for j in range(share):
         block_ref[pl.ds(r * share + j, 1), :] = rc_ref[j]
-    own_share = pl.ds(r * share, share)
     spread_rows(lambda to: block_ref.at[own_share], block_ref.at[own_share], 6)
-    spread_rows(lambda to: upper_ref.at[own_share], upper_ref.at[own_share], 7)
 
     all_bytes(rl_ref.at[pl.ds(0, cols - 1)], recv_sems.at[4]).wait()
     first = lax.broadcasted_iota(jnp.int32, (share // 2, LANES), 1) < half
@@ -304,7 +321,7 @@
     z = c // 2
     wz = wowners // 2
     plus, minus = zs // 2, zs - 1 - zs // 2
-    sib_plus, sib_minus = 2, 3
+    sib_plus, sib_minus = 4, 5
     away = lax.rem(z + 1, zs), lax.rem(z + zs - 1, zs)
 
     bases = (0, plus, plus + minus, plus + minus + sib_plus, zs + sib_plus + sib_minus - 1)
@@ -473,9 +490,13 @@
             jax.ShapeDtypeStruct((tall, count), f32),
             jax.ShapeDtypeStruct((weights.shape[0], count), bf16),
         ),
-        in_specs=[vmem] * 4,
+        in_specs=[pl.BlockSpec(memory_space=pl.ANY)] * 2 + [vmem],
         out_specs=(vmem,) * 3,
         scratch_shapes=[
+            pltpu.VMEM((tall, wide), f32),
+            pltpu.VMEM(weights.shape, bf16),
+            pltpu.VMEM((count, LANES), jnp.int32),
+            dma((2,)),
             pltpu.VMEM((count, count), f32),
             pltpu.VMEM((wide, count), f32),
             pltpu.VMEM((LANES, count), f32),
@@ -505,15 +526,68 @@
             flops=2 * tall * wide * LANES * 6, bytes_accessed=8 * 1024 * 1024, transcendentals=0
         ),
         name="exchange",
-    )(hess_inv, weights, removed.reshape(count // LANES, LANES), removed.reshape(count, 1))
+    )(hess_inv, weights, removed.reshape(count // LANES, LANES))
+
+
+def update_kernel(
+    hess_ref, weight_ref, left_ref, wleft_ref, coupling_ref, hess_out_ref, weight_out_ref, terms_ref
+):
+    count = coupling_ref.shape[0]
+
+    @pl.when(pl.program_id(0) == 0)
+    def _():
+        high, mid, _ = split3(coupling_ref[...])
+        terms_ref[0:count] = high
+        terms_ref[count : 2 * count] = mid
+        terms_ref[2 * count : 3 * count] = high
+
+    high, mid, _ = split3(left_ref[...])
+    hess_out_ref[...] = hess_ref[...] - jnp.dot(
+        jnp.concatenate([mid, high, high], axis=1),
+        terms_ref[...],
+        preferred_element_type=jnp.float32,
+    )
+    own = wleft_ref[...]
+    change = jnp.dot(
+        jnp.concatenate([own, own], axis=1),
+        terms_ref[count : 3 * count],
+        preferred_element_type=jnp.float32,
+    )
+    weight_out_ref[...] = (weight_ref[...].astype(jnp.float32) - change).astype(jnp.bfloat16)
+
+
+def update(hess_inv, weights, left, weight_left, coupling):
+    steps = 4
+    count, wide = coupling.shape
+    tall, high = hess_inv.shape[0] // steps, weights.shape[0] // steps
+
+    def rows_of(size, width):
+        return pl.BlockSpec((size, width), lambda i: (i, 0))
+
+    return pl.pallas_call(
+        update_kernel,
+        grid=(steps,),
+        out_shape=(
+            jax.ShapeDtypeStruct(hess_inv.shape, jnp.float32),
+            jax.ShapeDtypeStruct(weights.shape, jnp.bfloat16),
+        ),
+        in_specs=[
+            rows_of(tall, wide),
+            rows_of(high, wide),
+            rows_of(tall, count),
+            rows_of(high, count),
+            pl.BlockSpec((count, wide), lambda i: (0, 0)),
+        ],
+        out_specs=(rows_of(tall, wide), rows_of(high, wide)),
+        scratch_shapes=[pltpu.VMEM((3 * count, wide), jnp.bfloat16)],
+        compiler_params=pltpu.CompilerParams(vmem_limit_bytes=32 * 1024 * 1024),
+        name="update",
+    )(hess_inv, weights, left, weight_left, coupling)
 
 
 def on_device(hess_inv, weights, removed):
     coupling, left, weight_left = exchange(hess_inv, weights, removed)
-    hess_out = hess_inv - jnp.dot(left, coupling, precision=HIGHEST)
-    weight_fix = jnp.dot(weight_left.astype(jnp.float32), coupling, precision=HIGHEST)
-    weight_out = (weights.astype(jnp.float32) - weight_fix).astype(jnp.bfloat16)
-    return (hess_out, weight_out)
+    return update(hess_inv, weights, left, weight_left, coupling)
 
 
 def solution(mesh):

time: 117 us -> 105 us (0.90)
  matrix products: 6.48 us -> 0 us
  Pallas kernels: 107 us -> 101 us
    pallas_call x1, Pallas kernels: 107 us -> 97.4 us  [exchange(): pl.pallas_call(functools.partial(exchange_kernel, rows, cols), out_shape=...]
    dot_general x2 -> x0, matrix products: 6.48 us -> none  [the longest x1 4.87 us: on_device(): hess_out = hess_inv - jnp.dot(left, coupling, precision=HIGHEST)]
    pallas_call x0 -> x1, Pallas kernels: none -> 3.94 us  [update(): pl.pallas_call(update_kernel, grid=(steps,), out_shape=(jax.ShapeDtypeStr...]
    unnamed x6, local copies, waits for them, and re-layouts: 1.68 us -> 3.26 us
where the time goes in v3:
time: 105 us
  Pallas kernels  101 us (96%)
  local copies, waits for them, and re-layouts  3.26 us (3%)
    pallas_call x1, Pallas kernels, exchange(): pl.pallas_call(functools.partial(exchange_kernel, rows, cols), out_shape=...  97.4 us
    pallas_call x1, Pallas kernels, update(): pl.pallas_call(update_kernel, grid=(steps,), out_shape=(jax.ShapeDtypeStr...  3.94 us
    unnamed x6, local copies, waits for them, and re-layouts  3.26 us

profile of v3, /device:TPU:2, one launch (start us, length us, event | category | flops | bytes accessed | tf_op | source)
XLA Modules:
  0.0 105.2 jit_solution(10869058383149745647)
XLA Ops:
  0.6 0.0 copy-start
  0.6 1.6 %copy-done = f32[1024,512]{1,0:T(8,128)S(1)} copy-done((f32[1024,512]{1,0:T(8,128)S(1)}, f32[1024,512]{1,0:T(8,128)}, u32[]{:S(2)}) %copy-start) | copy-done | bytes 2097176
  2.2 0.0 copy-start.1
  2.2 1.0 copy-done.1
  3.2 0.0 copy-start.2
  3.2 0.7 copy-done.2
  3.9 97.4 %exchange.1 = (f32[512,512]{1,0:T(8,128)S(1)}, f32[1024,512]{1,0:T(8,128)S(1)}, bf16[384,512]{1,0:T(8,128)(2,1)S(1)}) custom-call(f32[1024,512]{1,0:T(8,128)S(1)} %copy-done, bf16[384,512]{1,0:T(8,128)(2,1)S(1)} %copy-done.1, s32[4,128]{1,0:T(4,128)S(1)} %bitcast.1), custom_call_target="tpu_custom_call" | custom-call | flops 805306368 | bytes 8388608 | tf_op jit(solution)/shard_map/exchange/pallas_call | solution.py:486
  101.3 3.9 %update.1 = (f32[1024,512]{1,0:T(8,128)}, bf16[384,512]{1,0:T(8,128)(2,1)}) custom-call(f32[1024,512]{1,0:T(8,128)S(1)} %copy-done, bf16[384,512]{1,0:T(8,128)(2,1)S(1)} %copy-done.1, f32[1024,512]{1,0:T(8,128)S(1)} %get-tuple-element.5.left_ref, bf16[384,512]{1,0:T(8,128)(2,1)S(1)} %get-tuple-element.6.wleft_ref, f32[512,512]{1,0:T(8,128)S(1)} %get-tuple-element.7.coupling_ref), custom_call_target="tpu_custom_call" | custom-call | tf_op jit(solution)/shard_map/update/pallas_call | solution.py:567
Async XLA Ops:
  0.6 1.6 %copy-start = (f32[1024,512]{1,0:T(8,128)S(1)}, f32[1024,512]{1,0:T(8,128)}, u32[]{:S(2)}) copy-start(f32[1024,512]{1,0:T(8,128)} %hess_ref.1) | copy-start | bytes 6291460
  2.2 1.0 copy-start.1
  3.2 0.7 copy-start.2

commit v4 on v3

--- a/solution.py
+++ b/solution.py
@@ -520,7 +520,7 @@
             dma((2 * zs,)),
         ],
         compiler_params=pltpu.CompilerParams(
-            collective_id=0, has_side_effects=True, vmem_limit_bytes=48 * 1024 * 1024
+            collective_id=0, has_side_effects=True, vmem_limit_bytes=60 * 1024 * 1024
         ),
         cost_estimate=pl.CostEstimate(
             flops=2 * tall * wide * LANES * 6, bytes_accessed=8 * 1024 * 1024, transcendentals=0
@@ -580,7 +580,7 @@
         ],
         out_specs=(rows_of(tall, wide), rows_of(high, wide)),
         scratch_shapes=[pltpu.VMEM((3 * count, wide), jnp.bfloat16)],
-        compiler_params=pltpu.CompilerParams(vmem_limit_bytes=32 * 1024 * 1024),
+        compiler_params=pltpu.CompilerParams(vmem_limit_bytes=60 * 1024 * 1024),
         name="update",
     )(hess_inv, weights, left, weight_left, coupling)
 

time: 105 us -> 107 us (1.019)
  Pallas kernels: 101 us -> 106 us
  local copies, waits for them, and re-layouts: 3.26 us -> 0 us
    unnamed x6 -> x0, local copies, waits for them, and re-layouts: 3.26 us -> none
    pallas_call x1, Pallas kernels: 3.94 us -> 6.47 us  [update(): pl.pallas_call(update_kernel, grid=(steps,), out_shape=(jax.ShapeDtypeStr...]
    pallas_call x1, Pallas kernels: 97.4 us -> 99.3 us  [exchange(): pl.pallas_call(functools.partial(exchange_kernel, rows, cols), out_shape=...]
where the time goes in v4:
time: 107 us; the launch traced here: 106 us
  Pallas kernels  106 us (99%)
    pallas_call x1, Pallas kernels, exchange(): pl.pallas_call(functools.partial(exchange_kernel, rows, cols), out_shape=...  99.3 us
    pallas_call x1, Pallas kernels, update(): pl.pallas_call(update_kernel, grid=(steps,), out_shape=(jax.ShapeDtypeStr...  6.47 us

profile of v4, /device:TPU:2, one launch (start us, length us, event | category | flops | bytes accessed | tf_op | source)
XLA Modules:
  0.0 106.4 jit_solution(2382925168901434562)
XLA Ops:
  0.6 99.3 %exchange.1 = (f32[512,512]{1,0:T(8,128)}, f32[1024,512]{1,0:T(8,128)}, bf16[384,512]{1,0:T(8,128)(2,1)}) custom-call(f32[1024,512]{1,0:T(8,128)} %hess_ref.1, bf16[384,512]{1,0:T(8,128)(2,1)} %weight_ref.1, s32[4,128]{1,0:T(4,128)} %bitcast.1), custom_call_target="tpu_custom_call" | custom-call | flops 805306368 | bytes 8388608 | tf_op jit(solution)/shard_map/exchange/pallas_call | solution.py:486
  99.9 6.5 %update.1 = (f32[1024,512]{1,0:T(8,128)}, bf16[384,512]{1,0:T(8,128)(2,1)}) custom-call(f32[1024,512]{1,0:T(8,128)} %hess_ref.1, bf16[384,512]{1,0:T(8,128)(2,1)} %weight_ref.1, f32[1024,512]{1,0:T(8,128)} %get-tuple-element.5.left_ref, bf16[384,512]{1,0:T(8,128)(2,1)} %get-tuple-element.6.wleft_ref, f32[512,512]{1,0:T(8,128)} %get-tuple-element.7.coupling_ref), custom_call_target="tpu_custom_call" | custom-call | tf_op jit(solution)/shard_map/update/pallas_call | solution.py:567
